TPU v7x, 512 devices: a whole 4x8x8 slice. The times are simulated.
512 devices in a mesh: dp: 64 (over y, z), cluster: 8 (over x, core).
Axes of the slice: x: 4, y: 8, z: 8, core: 2. Of those that a mesh axis runs over, the one named last changes fastest.
Arguments:
- embeddings: bfloat16 [32768, 1024], P('dp'), may hold values from -1 to 1, as said below
- centroids: bfloat16 [4096, 1024], P('cluster'), may hold values from -1 to 1, as said below
Outputs:
- refreshed_centroids: float32 [4096, 1024], P(('cluster', 'dp'))
- row_scale_logarithm: float32 [32768], P('dp')
- col_log_scale: float32 [4096], P('cluster')
Inputs may be any that keep to these rules, and one draw needn't show every extreme that they name: Every row of embeddings and of centroids has unit Euclidean length up to bfloat16 rounding. `centroids`: every row has unit Euclidean length up to bfloat16 rounding.
All inputs are finite; a program needn't handle non-finite values.
Results may differ from a plain program's by a relative error of at most 0.0014.
Values sent between devices are 32-bit elements; how exact they have to be, the bound alone decides.
A program may use at most 64 MiB of HBM per device.

v0:
```python
import jax
import jax.numpy as jnp
from jax import lax
from jax.sharding import PartitionSpec as P

ITERS = 3


SOFTMAX_TEMP = 0.1


def score_tile(embeddings, centroids):
    assignment_logits = lax.dot_general(
        embeddings, centroids, (((1,), (1,)), ((), ())), preferred_element_type=jnp.float32
    )
    return jnp.exp(assignment_logits / SOFTMAX_TEMP)


def per_device(embeddings, centroids):
    local_rows = embeddings.shape[0]
    local_cents = centroids.shape[0]
    row_shares_block = local_cents // lax.axis_size("dp")
    ratio = local_rows * lax.axis_size("dp") / (local_cents * lax.axis_size("cluster"))
    fetch = lambda: score_tile(embeddings, centroids)
    row_scale_factor = jnp.ones((local_rows,), jnp.float32)
    col_scale = jnp.ones((local_cents,), jnp.float32)
    for sweep in range(ITERS):
        column_part = jnp.sum(fetch() * row_scale_factor[:, None], axis=0)
        column_total = lax.psum(column_part, "dp")
        col_scale = ratio / column_total
        row_part = jnp.sum(fetch() * col_scale[None, :], axis=1)
        row_scale_factor = 1.0 / lax.psum(row_part, "cluster")
    plan = row_scale_factor[:, None] * fetch() * col_scale[None, :]
    mass_part = jnp.sum(plan, axis=0)
    plan_rounded = plan.astype(jnp.bfloat16)
    numerators = lax.psum_scatter(
        lax.dot_general(
            plan_rounded, embeddings, (((0,), (0,)), ((), ())), preferred_element_type=jnp.float32
        ),
        "dp",
        scatter_dimension=0,
        tiled=True,
    )
    mass_total = lax.psum(mass_part, "dp")
    mass_portion = lax.dynamic_slice_in_dim(
        mass_total, lax.axis_index("dp") * row_shares_block, row_shares_block
    )
    return (numerators / mass_portion[:, None], jnp.log(row_scale_factor), jnp.log(col_scale))


def solution(mesh):
    in_specs = (P("dp", None), P("cluster", None))
    out_specs = (P(("cluster", "dp"), None), P("dp"), P("cluster"))
    return jax.shard_map(
        per_device, mesh=mesh, in_specs=in_specs, out_specs=out_specs, check_vma=False
    )
```

profile of v0, /device:TPU:1, one launch (start us, length us, event | category | flops | bytes accessed | tf_op | source)
XLA Modules:
  0.0 639.2 jit_solution(1891073557672149994)
XLA Ops:
  7.2 0.0 copy-start
  7.2 0.0 all-reduce.3.cloned.1.call-start
  7.2 1.2 copy-done
  8.4 2.0 fusion.9
  10.4 123.3 %psum.49 = f32[512]{0:T(512)S(1)} all-reduce(f32[512]{0:T(512)S(1)} %get-tuple-element.7), channel_id=1, replica_groups=mesh['dp'=64,'cluster'=8] {'dp'}, use_global_device_ids=true, to_apply=%region_1.0 | all-reduce | flops 512 | bytes 4096 | tf_op jit(solution)/shard_map/psum | solution.py:29
  133.7 0.2 multiply_reduce_fusion.4
  133.8 39.9 %psum.50 = f32[512]{0:T(512)S(1)} all-reduce(f32[512]{0:T(512)S(1)} %multiply_reduce_fusion.4), channel_id=1, replica_groups=mesh['dp'=64,'cluster'=8] {'cluster'}, use_global_device_ids=true, to_apply=%region_3.0 | all-reduce | flops 512 | bytes 4096 | tf_op jit(solution)/shard_map/psum | solution.py:32
  173.7 0.2 multiply_reduce_fusion.3
  173.9 110.2 %psum.51 = f32[512]{0:T(512)S(1)} all-reduce(f32[512]{0:T(512)S(1)} %multiply_reduce_fusion.3), channel_id=1, replica_groups=mesh['dp'=64,'cluster'=8] {'dp'}, use_global_device_ids=true, to_apply=%region_5.0 | all-reduce | flops 512 | bytes 4096 | tf_op jit(solution)/shard_map/psum | solution.py:29
  284.1 0.2 multiply_reduce_fusion.2
  284.3 40.2 %psum.52 = f32[512]{0:T(512)S(1)} all-reduce(f32[512]{0:T(512)S(1)} %multiply_reduce_fusion.2), channel_id=1, replica_groups=mesh['dp'=64,'cluster'=8] {'cluster'}, use_global_device_ids=true, to_apply=%region_7.0 | all-reduce | flops 512 | bytes 4096 | tf_op jit(solution)/shard_map/psum | solution.py:32
  324.4 0.2 multiply_reduce_fusion.1
  324.6 112.1 %psum.53 = f32[512]{0:T(512)S(1)} all-reduce(f32[512]{0:T(512)S(1)} %multiply_reduce_fusion.1), channel_id=1, replica_groups=mesh['dp'=64,'cluster'=8] {'dp'}, use_global_device_ids=true, to_apply=%region_9.0 | all-reduce | flops 512 | bytes 4096 | tf_op jit(solution)/shard_map/psum | solution.py:29
  436.7 0.6 fusion.7
  437.3 0.1 multiply_reduce_fusion
  437.4 40.3 %psum.54 = f32[512]{0:T(512)S(1)} all-reduce(f32[512]{0:T(512)S(1)} %multiply_reduce_fusion), channel_id=1, replica_groups=mesh['dp'=64,'cluster'=8] {'cluster'}, use_global_device_ids=true, to_apply=%region_11.0 | all-reduce | flops 512 | bytes 4096 | tf_op jit(solution)/shard_map/psum | solution.py:32
  477.7 0.6 fusion.8
  478.3 2.1 fusion.3
  480.5 0.0 all-reduce.3.cloned.1.call-update
  480.5 0.2 fusion.1
  480.7 110.5 %psum.55 = f32[512]{0:T(512)S(1)} all-reduce(f32[512]{0:T(512)S(1)} %fusion.1), channel_id=1, replica_groups=mesh['dp'=64,'cluster'=8] {'dp'}, use_global_device_ids=true, to_apply=%region_14.0 | all-reduce | flops 512 | bytes 4096 | tf_op jit(solution)/shard_map/psum | solution.py:44
  591.2 0.1 dynamic_slice.3
  591.3 1.3 dynamic-slice
  593.2 37.7 %all-reduce.3.cloned.1.call-done = f32[512,1024]{1,0:T(8,128)} async-done(((f32[512,1024]{1,0:T(8,128)}), f32[512,1024]{1,0:T(8,128)}) %all-reduce.3.cloned.1.call-update) | async-done | bytes 2097168
  630.9 1.4 dynamic-slice_divide_fusion
  (4 shorter events, 0.0 us)
Async XLA Ops:
  7.2 1.2 copy-start
  7.2 623.7 %all-reduce.3.cloned.1.call-start = ((), (), s32[]{:S(2)}) async-start(), calls=%async_computation | async-start | bytes 4194304
Sparse Core Ops, SparseCore 0:
  480.6 150.2 all-reduce.2
where the time goes:
time: 642 us; the launch traced here: 639 us
  blocking collectives  576 us (90%)
  waiting for transfers between devices  37.7 us (6%)
  between operations  14.7 us (2%)
    psum x3, blocking collectives, per_device(): column_total = lax.psum(column_part, 'dp')  346 us
    psum x3, blocking collectives, per_device(): row_scale_factor = 1.0 / lax.psum(row_part, 'cluster')  120 us
    psum x1, blocking collectives, per_device(): mass_total = lax.psum(mass_part, 'dp')  111 us
    unnamed x2, waiting for transfers between devices  37.7 us
  transfers between devices with their start and end apart: 1, of which 1 were waited for; matrix products, arithmetic and copies ran while one was open for 0% of the time, Pallas kernels for 0%

commit v1 on v0

v1 whole, which is shorter than its diff:
```python
import functools

import jax
import jax.numpy as jnp
from jax import lax
from jax.experimental import pallas as pl
from jax.experimental.pallas import tpu as pltpu
from jax.sharding import PartitionSpec as P

ITERS = 3
INV_TEMP = 10.0
RATIO = 8.0
NY, NZ, NCL = 8, 8, 8
N, K, D = 512, 512, 1024
LANES = 128
T = N // LANES
HALF = D // 2
MESH = pl.DeviceIdType.MESH


def ring_dist(a, n=8):
    return min(a, n - a)


DP_OFFSETS = sorted(
    ((a, b) for a in range(NY) for b in range(NZ) if a or b),
    key=lambda p: -(ring_dist(p[0]) + ring_dist(p[1])),
)
RING_OFFSETS = (4, 3, 5, 2, 6, 1, 7)
CL_OFFSETS = (4, 5, 3, 2, 6, 7, 1)


def transposed_sum(p):
    return jnp.sum(p.T, axis=0, keepdims=True)


def weighted_sums(m_ref, v, put):
    for j in range(T):
        rows = slice(j * LANES, (j + 1) * LANES)
        p = m_ref[rows, 0:LANES] * v[0:1, :]
        for q in range(1, T):
            p += m_ref[rows, q * LANES : (q + 1) * LANES] * v[q : q + 1, :]
        put(j, transposed_sum(p))


def main_kernel(
    e_hbm, c_hbm, out_ref, r_ref, c_ref,
    e_ref, cent_ref, s_ref, st_ref, plan_ref, num_a, num_b, red_a, red_b,
    col_send, col_recv, row_send, row_recv, mass_send, mass_recv,
    got_a, got_b, fin_a, fin_b,
    load_sem, col_ssem, col_rsem, row_ssem, row_rsem, mass_sems, a_sems, b_sems, fa_sems, fb_sems,
):
    dp = lax.axis_index("dp")
    cl = lax.axis_index("cluster")
    y, z = dp // NZ, lax.rem(dp, NZ)

    def dp_dev(dy, dz):
        return lax.rem(y + dy, NY) * NZ + lax.rem(z + dz, NZ)

    load_e = pltpu.make_async_copy(e_hbm, e_ref, load_sem.at[0])
    load_c = pltpu.make_async_copy(c_hbm, cent_ref, load_sem.at[1])
    load_e.start()
    load_c.start()

    barrier = pltpu.get_barrier_semaphore()
    for dy, dz in DP_OFFSETS:
        pl.semaphore_signal(barrier, inc=1, device_id=(dp_dev(dy, dz), cl), device_id_type=MESH)
    for j in CL_OFFSETS:
        pl.semaphore_signal(barrier, inc=1, device_id=(dp, lax.rem(cl + j, NCL)), device_id_type=MESH)

    load_e.wait()
    load_c.wait()
    nt = (((1,), (1,)), ((), ()))
    for j in range(T):
        rows = slice(j * LANES, (j + 1) * LANES)
        st_ref[rows, :] = jnp.exp(
            lax.dot_general(cent_ref[rows, :], e_ref[...], nt, preferred_element_type=jnp.float32) * INV_TEMP
        )
    for j in range(T):
        rows = slice(j * LANES, (j + 1) * LANES)
        s_ref[rows, :] = jnp.exp(
            lax.dot_general(e_ref[rows, :], cent_ref[...], nt, preferred_element_type=jnp.float32) * INV_TEMP
        )
    pl.semaphore_wait(barrier, len(DP_OFFSETS) + len(CL_OFFSETS))

    def total_wait(buf, sem):
        pltpu.make_async_copy(buf, buf, sem).wait()

    def iteration(it, r):
        def put_col(j, v):
            col_send[it, j : j + 1, :] = v

        weighted_sums(st_ref, r, put_col)
        for i, (dy, dz) in enumerate(DP_OFFSETS):
            pltpu.make_async_remote_copy(
                col_send.at[it], col_recv.at[it, i], col_ssem.at[it], col_rsem.at[it],
                device_id=(dp_dev(dy, dz), cl), device_id_type=MESH,
            ).start()
        total_wait(col_recv.at[it], col_rsem.at[it])
        c = RATIO / (col_send[it] + jnp.sum(col_recv[it], axis=0))
        c_ref[...] = c

        def put_row(j, v):
            row_send[it, j : j + 1, :] = v

        weighted_sums(s_ref, c, put_row)
        for i, j in enumerate(CL_OFFSETS):
            pltpu.make_async_remote_copy(
                row_send.at[it], row_recv.at[it, i], row_ssem.at[it], row_rsem.at[it],
                device_id=(dp, lax.rem(cl + j, NCL)), device_id_type=MESH,
            ).start()

        @pl.when(it == ITERS - 1)
        def _():
            for j in range(T):
                rows = slice(j * LANES, (j + 1) * LANES)
                c_col = jnp.broadcast_to(c[j : j + 1, :], (LANES, LANES)).T
                for q in range(T):
                    cols = slice(q * LANES, (q + 1) * LANES)
                    st_ref[rows, cols] = st_ref[rows, cols] * c_col

        total_wait(row_recv.at[it], row_rsem.at[it])
        return 1.0 / (row_send[it] + jnp.sum(row_recv[it], axis=0))

    r = lax.fori_loop(0, ITERS, iteration, jnp.ones((T, LANES), jnp.float32))
    r_ref[...] = r

    for j in range(T):
        rows = slice(j * LANES, (j + 1) * LANES)
        p = None
        for q in range(T):
            cols = slice(q * LANES, (q + 1) * LANES)
            plan = st_ref[rows, cols] * r[q : q + 1, :]
            p = plan if p is None else p + plan
            plan_ref[rows, cols] = plan.astype(jnp.bfloat16)
        mass_send[j] = transposed_sum(p)

    num_a[...] = jnp.dot(
        plan_ref[...], e_ref[:, :HALF], preferred_element_type=jnp.float32
    ).reshape(NY, NZ, 8, HALF)
    for dy in RING_OFFSETS:
        pltpu.make_async_remote_copy(
            num_a.at[lax.rem(y + dy, NY)], got_a.at[dy - 1], a_sems.at[0], a_sems.at[1],
            device_id=(dp_dev(dy, 0), cl), device_id_type=MESH,
        ).start()
    num_b[...] = jnp.dot(
        plan_ref[...], e_ref[:, HALF:], preferred_element_type=jnp.float32
    ).reshape(NY, NZ, 8, HALF)
    for dz in RING_OFFSETS:
        pltpu.make_async_remote_copy(
            num_b.at[:, lax.rem(z + dz, NZ)], got_b.at[dz - 1], b_sems.at[0], b_sems.at[1],
            device_id=(dp_dev(0, dz), cl), device_id_type=MESH,
        ).start()
    for i, (dy, dz) in enumerate(DP_OFFSETS):
        owner = dp_dev(dy, dz)
        pltpu.make_async_remote_copy(
            mass_send.at[owner // (LANES // 8)], mass_recv.at[i], mass_sems.at[0], mass_sems.at[1],
            device_id=(owner, cl), device_id_type=MESH,
        ).start()

    total_wait(got_a, a_sems.at[1])
    for k in range(8):
        red_a[k] = num_a[y, k] + jnp.sum(got_a[:, k], axis=0)
    for dz in RING_OFFSETS:
        pltpu.make_async_remote_copy(
            red_a.at[lax.rem(z + dz, NZ)], fin_a.at[dz - 1], fa_sems.at[0], fa_sems.at[1],
            device_id=(dp_dev(0, dz), cl), device_id_type=MESH,
        ).start()
    total_wait(got_b, b_sems.at[1])
    for k in range(8):
        red_b[k] = num_b[k, z] + jnp.sum(got_b[:, k], axis=0)
    for dy in RING_OFFSETS:
        pltpu.make_async_remote_copy(
            red_b.at[lax.rem(y + dy, NY)], fin_b.at[dy - 1], fb_sems.at[0], fb_sems.at[1],
            device_id=(dp_dev(dy, 0), cl), device_id_type=MESH,
        ).start()

    total_wait(mass_recv, mass_sems.at[1])
    mass_row = mass_send[dp // (LANES // 8)] + jnp.sum(mass_recv[...], axis=0)
    mine = lax.broadcasted_iota(jnp.int32, (8, LANES), 1) == (
        lax.rem(dp, LANES // 8) * 8 + lax.broadcasted_iota(jnp.int32, (8, LANES), 0)
    )
    mass = jnp.sum(jnp.where(mine, jnp.broadcast_to(mass_row, (8, LANES)), 0.0), axis=1, keepdims=True)

    total_wait(fin_a, fa_sems.at[1])
    out_ref[:, :HALF] = (red_a[z] + jnp.sum(fin_a[...], axis=0)) / mass
    total_wait(fin_b, fb_sems.at[1])
    out_ref[:, HALF:] = (red_b[y] + jnp.sum(fin_b[...], axis=0)) / mass

    for it in range(ITERS):
        total_wait(col_recv.at[it], col_ssem.at[it])
        total_wait(row_recv.at[it], row_ssem.at[it])
    total_wait(got_a, a_sems.at[0])
    total_wait(got_b, b_sems.at[0])
    total_wait(mass_recv, mass_sems.at[0])
    total_wait(fin_a, fa_sems.at[0])
    total_wait(fin_b, fb_sems.at[0])


def finish_kernel(num_ref, r_ref, c_ref, out_ref, lr_ref, lc_ref):
    out_ref[...] = num_ref[...]
    lr_ref[...] = jnp.log(r_ref[...])
    lc_ref[...] = jnp.log(c_ref[...])


def per_device(embeddings, centroids):
    f32 = jnp.float32
    vmem = pl.BlockSpec(memory_space=pltpu.VMEM)
    hbm = pl.BlockSpec(memory_space=pl.ANY)
    dma = pltpu.SemaphoreType.DMA
    outs = (
        jax.ShapeDtypeStruct((8, D), f32),
        jax.ShapeDtypeStruct((T, LANES), f32),
        jax.ShapeDtypeStruct((T, LANES), f32),
    )
    n_dp, n_cl = len(DP_OFFSETS), len(CL_OFFSETS)
    num, r, c = pl.pallas_call(
        main_kernel,
        out_shape=outs,
        in_specs=[hbm, hbm],
        out_specs=(vmem, vmem, vmem),
        scratch_shapes=[
            pltpu.VMEM((N, D), jnp.bfloat16),
            pltpu.VMEM((K, D), jnp.bfloat16),
            pltpu.VMEM((N, K), f32),
            pltpu.VMEM((K, N), f32),
            pltpu.VMEM((K, N), jnp.bfloat16),
            pltpu.VMEM((NY, NZ, 8, HALF), f32),
            pltpu.VMEM((NY, NZ, 8, HALF), f32),
            pltpu.VMEM((NZ, 8, HALF), f32),
            pltpu.VMEM((NY, 8, HALF), f32),
            pltpu.VMEM((ITERS, T, LANES), f32),
            pltpu.VMEM((ITERS, n_dp, T, LANES), f32),
            pltpu.VMEM((ITERS, T, LANES), f32),
            pltpu.VMEM((ITERS, n_cl, T, LANES), f32),
            pltpu.VMEM((T, 1, LANES), f32),
            pltpu.VMEM((n_dp, 1, LANES), f32),
            pltpu.VMEM((NY - 1, NZ, 8, HALF), f32),
            pltpu.VMEM((NZ - 1, NY, 8, HALF), f32),
            pltpu.VMEM((NZ - 1, 8, HALF), f32),
            pltpu.VMEM((NY - 1, 8, HALF), f32),
            dma((2,)),
            dma((ITERS,)),
            dma((ITERS,)),
            dma((ITERS,)),
            dma((ITERS,)),
            dma((2,)),
            dma((2,)),
            dma((2,)),
            dma((2,)),
            dma((2,)),
        ],
        compiler_params=pltpu.CompilerParams(
            collective_id=0, has_side_effects=True, vmem_limit_bytes=48 * 2**20
        ),
    )(embeddings, centroids)
    out, lr, lc = pl.pallas_call(
        finish_kernel, out_shape=outs, in_specs=[vmem] * 3, out_specs=(vmem,) * 3
    )(num, r, c)
    return out, lr.reshape(N), lc.reshape(K)


def solution(mesh):
    in_specs = (P("dp", None), P("cluster", None))
    out_specs = (P(("cluster", "dp"), None), P("dp"), P("cluster"))
    return jax.shard_map(
        per_device, mesh=mesh, in_specs=in_specs, out_specs=out_specs, check_vma=False
    )
```

time: 642 us -> 88.8 us (0.14)
  blocking collectives: 576 us -> 0 us
  Pallas kernels: 0 us -> 83.7 us
  waiting for transfers between devices: 37.7 us -> 0 us
  between operations: 14.7 us -> 0.66 us
    psum x7 -> x0, blocking collectives: 576 us -> none  [the longest x3 346 us: per_device(): column_total = lax.psum(column_part, 'dp')]
    pallas_call x0 -> x2, Pallas kernels: none -> 83.7 us  [the longest x1 82.3 us: per_device(): pl.pallas_call(main_kernel, out_shape=outs, in_specs=[hbm, hbm], out_spec...]
    unnamed x2 -> x0, waiting for transfers between devices: 37.7 us -> none
  transfers between devices with their start and end apart: 1 -> 0, of which waited for: 1 -> 0; matrix products, arithmetic and copies ran while one was open for 0% -> 0% of each run, Pallas kernels for 0% -> 0%
where the time goes in v1:
time: 88.8 us; the launch traced here: 88.5 us
  Pallas kernels  83.7 us (94%)
  local copies, waits for them, and re-layouts  4.2 us (5%)
    pallas_call x1, Pallas kernels, per_device(): pl.pallas_call(main_kernel, out_shape=outs, in_specs=[hbm, hbm], out_spec...  82.3 us
    unnamed x10, local copies, waits for them, and re-layouts  4.2 us

profile of v1, /device:TPU:1, one launch (start us, length us, event | category | flops | bytes accessed | tf_op | source)
XLA Modules:
  0.0 88.5 jit_solution(3041156263724566741)
XLA Ops:
  0.6 0.0 copy-start
  0.6 1.2 %copy-done = bf16[512,1024]{1,0:T(8,128)(2,1)S(1)} copy-done((bf16[512,1024]{1,0:T(8,128)(2,1)S(1)}, bf16[512,1024]{1,0:T(8,128)(2,1)}, u32[]{:S(2)}) %copy-start) | copy-done | bytes 1048600
  1.9 0.0 copy-start.1
  1.9 1.2 %copy-done.1 = bf16[512,1024]{1,0:T(8,128)(2,1)S(1)} copy-done((bf16[512,1024]{1,0:T(8,128)(2,1)S(1)}, bf16[512,1024]{1,0:T(8,128)(2,1)}, u32[]{:S(2)}) %copy-start.1) | copy-done | bytes 1048600
  3.1 82.3 %shard_map.49 = (f32[8,1024]{1,0:T(8,128)S(1)}, f32[4,128]{1,0:T(4,128)S(1)}, f32[4,128]{1,0:T(4,128)S(1)}) custom-call(bf16[512,1024]{1,0:T(8,128)(2,1)S(1)} %copy-done, bf16[512,1024]{1,0:T(8,128)(2,1)S(1)} %copy-done.1), custom_call_target="tpu_custom_call" | custom-call | tf_op jit(solution)/shard_map/pallas_call | solution.py:217
  85.4 0.0 copy-start.2
  85.4 0.6 copy-done.2
  86.0 0.0 copy-start.3
  86.0 0.6 copy-done.3
  86.6 0.0 copy-start.4
  86.6 0.6 copy-done.4
  87.1 1.4 %shard_map.50 = (f32[8,1024]{1,0:T(8,128)}, f32[4,128]{1,0:T(4,128)}, f32[4,128]{1,0:T(4,128)}) custom-call(f32[8,1024]{1,0:T(8,128)} %copy-done.2, f32[4,128]{1,0:T(4,128)} %copy-done.3, f32[4,128]{1,0:T(4,128)} %copy-done.4), custom_call_target="tpu_custom_call" | custom-call | tf_op jit(solution)/shard_map/pallas_call | solution.py:257
Async XLA Ops:
  0.6 1.2 %copy-start = (bf16[512,1024]{1,0:T(8,128)(2,1)S(1)}, bf16[512,1024]{1,0:T(8,128)(2,1)}, u32[]{:S(2)}) copy-start(bf16[512,1024]{1,0:T(8,128)(2,1)} %e_hbm.1) | copy-start | bytes 3145732
  1.9 1.2 %copy-start.1 = (bf16[512,1024]{1,0:T(8,128)(2,1)S(1)}, bf16[512,1024]{1,0:T(8,128)(2,1)}, u32[]{:S(2)}) copy-start(bf16[512,1024]{1,0:T(8,128)(2,1)} %c_hbm.1) | copy-start | bytes 3145732
  85.4 0.6 copy-start.2
  86.0 0.6 copy-start.3
  86.6 0.6 copy-start.4

commit v2 on v1

v2 whole, which is shorter than its diff:
```python
import functools

import jax
import jax.numpy as jnp
from jax import lax
from jax.experimental import pallas as pl
from jax.experimental.pallas import tpu as pltpu
from jax.sharding import PartitionSpec as P

ITERS = 3
INV_TEMP = 10.0
RATIO = 8.0
NY, NZ, NCL = 8, 8, 8
N, K, D = 512, 512, 1024
LANES = 128
T = N // LANES
HALF = D // 2
CHUNKS = 2
W = HALF // CHUNKS
STEPS = 4
VMEM_LIMIT = 63 * 2**20
MESH = pl.DeviceIdType.MESH


def ring_dist(a, n=8):
    return min(a, n - a)


DP_OFFSETS = sorted(
    ((a, b) for a in range(NY) for b in range(NZ) if a or b),
    key=lambda p: -(ring_dist(p[0]) + ring_dist(p[1])),
)
RING_OFFSETS = (4, 3, 5, 2, 6, 1, 7)
CL_OFFSETS = (4, 5, 3, 2, 6, 7, 1)


def transposed_sum(p):
    return jnp.sum(p.T, axis=0, keepdims=True)


def weighted_sums(m_ref, v, put):
    for j in range(T):
        rows = slice(j * LANES, (j + 1) * LANES)
        p = m_ref[rows, 0:LANES] * v[0:1, :]
        for q in range(1, T):
            p += m_ref[rows, q * LANES : (q + 1) * LANES] * v[q : q + 1, :]
        put(j, transposed_sum(p))


def main_kernel(
    e_hbm, c_hbm, out_ref,
    e_ref, cent_ref, s_ref, st_ref, plan_ref, num, got, red, fin,
    col_send, col_recv, row_send, row_recv, mass_send, mass_recv,
    load_sem, col_ssem, col_rsem, row_ssem, row_rsem, mass_sems, ring_ssem, ring_rsem, fin_ssem, fin_rsem,
):
    dp = lax.axis_index("dp")
    cl = lax.axis_index("cluster")
    y, z = dp // NZ, lax.rem(dp, NZ)

    def dp_dev(dy, dz):
        return lax.rem(y + dy, NY) * NZ + lax.rem(z + dz, NZ)

    load_e = pltpu.make_async_copy(e_hbm, e_ref, load_sem.at[0])
    load_c = pltpu.make_async_copy(c_hbm, cent_ref, load_sem.at[1])
    load_e.start()
    load_c.start()

    barrier = pltpu.get_barrier_semaphore()
    for dy, dz in DP_OFFSETS:
        pl.semaphore_signal(barrier, inc=1, device_id=(dp_dev(dy, dz), cl), device_id_type=MESH)
    for j in CL_OFFSETS:
        pl.semaphore_signal(barrier, inc=1, device_id=(dp, lax.rem(cl + j, NCL)), device_id_type=MESH)

    load_e.wait()
    load_c.wait()
    nt = (((1,), (1,)), ((), ()))

    def score_rows(j, _):
        rows = pl.ds(pl.multiple_of(j * LANES, LANES), LANES)
        st_ref[rows, :] = jnp.exp(
            lax.dot_general(cent_ref[rows, :], e_ref[...], nt, preferred_element_type=jnp.float32) * INV_TEMP
        )
        s_ref[rows, :] = jnp.exp(
            lax.dot_general(e_ref[rows, :], cent_ref[...], nt, preferred_element_type=jnp.float32) * INV_TEMP
        )
        return 0

    lax.fori_loop(0, T, score_rows, 0)
    pl.semaphore_wait(barrier, len(DP_OFFSETS) + len(CL_OFFSETS))

    def total_wait(buf, sem):
        pltpu.make_async_copy(buf, buf, sem).wait()

    def iteration(it, r):
        def put_col(j, v):
            col_send[it, j : j + 1, :] = v

        weighted_sums(st_ref, r, put_col)
        for i, (dy, dz) in enumerate(DP_OFFSETS):
            pltpu.make_async_remote_copy(
                col_send.at[it], col_recv.at[it, i], col_ssem.at[it], col_rsem.at[it],
                device_id=(dp_dev(dy, dz), cl), device_id_type=MESH,
            ).start()
        total_wait(col_recv.at[it], col_rsem.at[it])
        c = RATIO / (col_send[it] + jnp.sum(col_recv[it], axis=0))
        out_ref[NZ, T : 2 * T, :] = c

        def put_row(j, v):
            row_send[it, j : j + 1, :] = v

        weighted_sums(s_ref, c, put_row)
        for i, j in enumerate(CL_OFFSETS):
            pltpu.make_async_remote_copy(
                row_send.at[it], row_recv.at[it, i], row_ssem.at[it], row_rsem.at[it],
                device_id=(dp, lax.rem(cl + j, NCL)), device_id_type=MESH,
            ).start()

        @pl.when(it == ITERS - 1)
        def _():
            for j in range(T):
                rows = slice(j * LANES, (j + 1) * LANES)
                c_col = jnp.broadcast_to(c[j : j + 1, :], (LANES, LANES)).T
                for q in range(T):
                    cols = slice(q * LANES, (q + 1) * LANES)
                    st_ref[rows, cols] = st_ref[rows, cols] * c_col

        total_wait(row_recv.at[it], row_rsem.at[it])
        return 1.0 / (row_send[it] + jnp.sum(row_recv[it], axis=0))

    r = lax.fori_loop(0, ITERS, iteration, jnp.ones((T, LANES), jnp.float32))
    out_ref[NZ, 0:T, :] = r

    for j in range(T):
        rows = slice(j * LANES, (j + 1) * LANES)
        p = None
        for q in range(T):
            cols = slice(q * LANES, (q + 1) * LANES)
            plan = st_ref[rows, cols] * r[q : q + 1, :]
            p = plan if p is None else p + plan
            plan_ref[rows, cols] = plan.astype(jnp.bfloat16)
        mass_send[j] = transposed_sum(p)

    for i, (dy, dz) in enumerate(DP_OFFSETS):
        owner = dp_dev(dy, dz)
        pltpu.make_async_remote_copy(
            mass_send.at[owner // (LANES // 8)], mass_recv.at[i], mass_sems.at[0], mass_sems.at[1],
            device_id=(owner, cl), device_id_type=MESH,
        ).start()

    place = (y, z)
    other = (z, y)

    def device_at(h, step, along):
        shift = (step, 0) if (h == 0) == along else (0, step)
        return (dp_dev(*shift), cl)

    def ring_send(h, ch, way, s):
        if s == 1:
            owner = lax.rem(place[h] + 4, 8)
            part = pl.ds(4 * way, 4)
        else:
            owner = lax.rem(place[h] + (3 + s if way == 0 else 5 - s), 8)
            part = pl.ds(0, 8)
        pltpu.make_async_remote_copy(
            num.at[h, ch, owner, part], got.at[h, way, ch, s - 1, part],
            ring_ssem.at[h, way, ch], ring_rsem.at[h, way, ch, s - 1],
            device_id=device_at(h, 7 if way == 0 else 1, True), device_id_type=MESH,
        ).start()

    def ring_take(h, ch, way, s):
        part = pl.ds(4 * way, 4) if s == 1 else pl.ds(0, 8)
        total_wait(got.at[h, way, ch, s - 1, part], ring_rsem.at[h, way, ch, s - 1])
        owner = lax.rem(place[h] + (4 + s if way == 0 else 4 - s), 8)
        num[h, ch, owner, part] += got[h, way, ch, s - 1, part]

    for ch in range(CHUNKS):
        for h in range(2):
            cols = slice(h * HALF + ch * W, h * HALF + (ch + 1) * W)
            block = jnp.dot(plan_ref[...], e_ref[:, cols], preferred_element_type=jnp.float32).reshape(8, 8, 8, W)
            if h == 0:
                num[h, ch] = block
            else:
                for k in range(8):
                    num[h, ch, :, k] = block[k]
            for way in range(2):
                ring_send(h, ch, way, 1)
    for s in range(1, STEPS):
        for ch in range(CHUNKS):
            for h in range(2):
                for way in range(2):
                    ring_take(h, ch, way, s)
                    ring_send(h, ch, way, s + 1)
    for ch in range(CHUNKS):
        for h in range(2):
            for way in range(2):
                ring_take(h, ch, way, STEPS)
            red[h, ch] = num[h, ch, place[h]]
            for d in RING_OFFSETS:
                pltpu.make_async_remote_copy(
                    red.at[h, ch, lax.rem(other[h] + d, 8)], fin.at[h, ch, d - 1], fin_ssem.at[h, ch], fin_rsem.at[h, ch],
                    device_id=device_at(h, d, False), device_id_type=MESH,
                ).start()

    total_wait(mass_recv, mass_sems.at[1])
    mass_row = mass_send[dp // (LANES // 8)] + jnp.sum(mass_recv[...], axis=0)
    mine = lax.broadcasted_iota(jnp.int32, (8, LANES), 1) == (
        lax.rem(dp, LANES // 8) * 8 + lax.broadcasted_iota(jnp.int32, (8, LANES), 0)
    )
    mass = jnp.sum(jnp.where(mine, jnp.broadcast_to(mass_row, (8, LANES)), 0.0), axis=1, keepdims=True)
    for ch in range(CHUNKS):
        for h in range(2):
            total_wait(fin.at[h, ch], fin_rsem.at[h, ch])
            block = (red[h, ch, other[h]] + jnp.sum(fin[h, ch], axis=0)) / mass
            for q in range(W // LANES):
                out_ref[(h * HALF + ch * W) // LANES + q] = block[:, q * LANES : (q + 1) * LANES]

    for it in range(ITERS):
        total_wait(col_recv.at[it], col_ssem.at[it])
        total_wait(row_recv.at[it], row_ssem.at[it])
    total_wait(mass_recv, mass_sems.at[0])
    for h in range(2):
        for ch in range(CHUNKS):
            total_wait(fin.at[h, ch], fin_ssem.at[h, ch])
            for way in range(2):
                total_wait(got.at[h, way, ch, pl.ds(0, 3)], ring_ssem.at[h, way, ch])
                total_wait(got.at[h, way, ch, 3, pl.ds(0, 4)], ring_ssem.at[h, way, ch])


def finish_kernel(all_ref, out_ref, lr_ref, lc_ref):
    for j in range(D // LANES):
        out_ref[:, j * LANES : (j + 1) * LANES] = all_ref[j]
    lr_ref[...] = jnp.log(all_ref[NZ, 0:T, :])
    lc_ref[...] = jnp.log(all_ref[NZ, T : 2 * T, :])


def per_device(embeddings, centroids):
    f32 = jnp.float32
    vmem = pl.BlockSpec(memory_space=pltpu.VMEM)
    hbm = pl.BlockSpec(memory_space=pl.ANY)
    dma = pltpu.SemaphoreType.DMA
    outs = (
        jax.ShapeDtypeStruct((8, D), f32),
        jax.ShapeDtypeStruct((T, LANES), f32),
        jax.ShapeDtypeStruct((T, LANES), f32),
    )
    n_dp, n_cl = len(DP_OFFSETS), len(CL_OFFSETS)
    packed = pl.pallas_call(
        main_kernel,
        out_shape=jax.ShapeDtypeStruct((D // LANES + 1, 8, LANES), f32),
        in_specs=[hbm, hbm],
        out_specs=vmem,
        scratch_shapes=[
            pltpu.VMEM((N, D), jnp.bfloat16),
            pltpu.VMEM((K, D), jnp.bfloat16),
            pltpu.VMEM((N, K), f32),
            pltpu.VMEM((K, N), f32),
            pltpu.VMEM((K, N), jnp.bfloat16),
            pltpu.VMEM((2, CHUNKS, 8, 8, 8, W), f32),
            pltpu.VMEM((2, 2, CHUNKS, STEPS, 8, 8, W), f32),
            pltpu.VMEM((2, CHUNKS, 8, 8, W), f32),
            pltpu.VMEM((2, CHUNKS, 7, 8, W), f32),
            pltpu.VMEM((ITERS, T, LANES), f32),
            pltpu.VMEM((ITERS, n_dp, T, LANES), f32),
            pltpu.VMEM((ITERS, T, LANES), f32),
            pltpu.VMEM((ITERS, n_cl, T, LANES), f32),
            pltpu.VMEM((T, 1, LANES), f32),
            pltpu.VMEM((n_dp, 1, LANES), f32),
            dma((2,)),
            dma((ITERS,)),
            dma((ITERS,)),
            dma((ITERS,)),
            dma((ITERS,)),
            dma((2,)),
            dma((2, 2, CHUNKS)),
            dma((2, 2, CHUNKS, STEPS)),
            dma((2, CHUNKS)),
            dma((2, CHUNKS)),
        ],
        compiler_params=pltpu.CompilerParams(
            collective_id=0, has_side_effects=True, vmem_limit_bytes=VMEM_LIMIT
        ),
    )(embeddings, centroids)
    out, lr, lc = pl.pallas_call(
        finish_kernel, out_shape=outs, in_specs=[vmem], out_specs=(vmem,) * 3,
        compiler_params=pltpu.CompilerParams(vmem_limit_bytes=2**20),
    )(packed)
    return out, lr.reshape(N), lc.reshape(K)


def solution(mesh):
    in_specs = (P("dp", None), P("cluster", None))
    out_specs = (P(("cluster", "dp"), None), P("dp"), P("cluster"))
    return jax.shard_map(
        per_device, mesh=mesh, in_specs=in_specs, out_specs=out_specs, check_vma=False
    )
```

time: 88.8 us -> 75.9 us (0.85)
  the two profiles are of different devices: /device:TPU:1 before, /device:TPU:8 now
where the time goes in v2:
time: 75.9 us; the launch traced here: 75.7 us
  Pallas kernels  74.3 us (98%)
  local copies, waits for them, and re-layouts  0.76 us (1%)
    pallas_call x1, Pallas kernels, per_device(): pl.pallas_call(main_kernel, out_shape=jax.ShapeDtypeStruct((D // LANES +...  73.6 us

profile of v2, /device:TPU:8, one launch (start us, length us, event | category | flops | bytes accessed | tf_op | source)
XLA Modules:
  0.0 75.7 jit_solution(16777278742667965429)
XLA Ops:
  0.6 73.6 %shard_map.49.all_ref = f32[9,8,128]{2,1,0:T(8,128)} custom-call(bf16[512,1024]{1,0:T(8,128)(2,1)} %e_hbm.1, bf16[512,1024]{1,0:T(8,128)(2,1)} %c_hbm.1), custom_call_target="tpu_custom_call" | custom-call | tf_op jit(solution)/shard_map/pallas_call | solution.py:247
  74.3 0.0 copy-start
  74.3 0.8 %copy-done = f32[9,8,128]{2,1,0:T(8,128)S(1)} copy-done((f32[9,8,128]{2,1,0:T(8,128)S(1)}, f32[9,8,128]{2,1,0:T(8,128)}, u32[]{:S(2)}) %copy-start) | copy-done | bytes 36888
  75.0 0.6 shard_map.50
Async XLA Ops:
  74.3 0.8 %copy-start = (f32[9,8,128]{2,1,0:T(8,128)S(1)}, f32[9,8,128]{2,1,0:T(8,128)}, u32[]{:S(2)}) copy-start(f32[9,8,128]{2,1,0:T(8,128)} %shard_map.49.all_ref) | copy-start | bytes 110596

commit v3 on v2

--- a/solution.py
+++ b/solution.py
@@ -15,10 +15,10 @@
 LANES = 128
 T = N // LANES
 HALF = D // 2
-CHUNKS = 2
+CHUNKS = 4
 W = HALF // CHUNKS
-STEPS = 4
-VMEM_LIMIT = 63 * 2**20
+SLOTS = 4
+VMEM_LIMIT = 267 * 2**20 // 5
 MESH = pl.DeviceIdType.MESH
 
 
@@ -140,13 +140,6 @@
             plan_ref[rows, cols] = plan.astype(jnp.bfloat16)
         mass_send[j] = transposed_sum(p)
 
-    for i, (dy, dz) in enumerate(DP_OFFSETS):
-        owner = dp_dev(dy, dz)
-        pltpu.make_async_remote_copy(
-            mass_send.at[owner // (LANES // 8)], mass_recv.at[i], mass_sems.at[0], mass_sems.at[1],
-            device_id=(owner, cl), device_id_type=MESH,
-        ).start()
-
     place = (y, z)
     other = (z, y)
 
@@ -154,24 +147,25 @@
         shift = (step, 0) if (h == 0) == along else (0, step)
         return (dp_dev(*shift), cl)
 
-    def ring_send(h, ch, way, s):
-        if s == 1:
-            owner = lax.rem(place[h] + 4, 8)
-            part = pl.ds(4 * way, 4)
-        else:
-            owner = lax.rem(place[h] + (3 + s if way == 0 else 5 - s), 8)
-            part = pl.ds(0, 8)
+    def ring_part(way, slot):
+        return pl.ds(4 * way, 4) if slot == 0 else pl.ds(0, 8)
+
+    def ring_owner(h, way, distance):
+        return lax.rem(place[h] + (8 - distance if way == 0 else distance), 8)
+
+    def ring_send(h, ch, way, slot):
+        hops = 2 if slot == 0 else 1
+        owner, part = ring_owner(h, way, 4 - slot), ring_part(way, slot)
         pltpu.make_async_remote_copy(
-            num.at[h, ch, owner, part], got.at[h, way, ch, s - 1, part],
-            ring_ssem.at[h, way, ch], ring_rsem.at[h, way, ch, s - 1],
-            device_id=device_at(h, 7 if way == 0 else 1, True), device_id_type=MESH,
+            num.at[h, ch, owner, part], got.at[h, way, ch, slot, part],
+            ring_ssem.at[h, way, ch], ring_rsem.at[h, way, ch, slot],
+            device_id=device_at(h, 8 - hops if way == 0 else hops, True), device_id_type=MESH,
         ).start()
 
-    def ring_take(h, ch, way, s):
-        part = pl.ds(4 * way, 4) if s == 1 else pl.ds(0, 8)
-        total_wait(got.at[h, way, ch, s - 1, part], ring_rsem.at[h, way, ch, s - 1])
-        owner = lax.rem(place[h] + (4 + s if way == 0 else 4 - s), 8)
-        num[h, ch, owner, part] += got[h, way, ch, s - 1, part]
+    def ring_take(h, ch, way, slot):
+        part = ring_part(way, slot)
+        total_wait(got.at[h, way, ch, slot, part], ring_rsem.at[h, way, ch, slot])
+        num[h, ch, ring_owner(h, way, min(2, 3 - slot)), part] += got[h, way, ch, slot, part]
 
     for ch in range(CHUNKS):
         for h in range(2):
@@ -182,18 +176,28 @@
             else:
                 for k in range(8):
                     num[h, ch, :, k] = block[k]
-            for way in range(2):
-                ring_send(h, ch, way, 1)
-    for s in range(1, STEPS):
+            for slot in range(2):
+                for way in range(2):
+                    ring_send(h, ch, way, slot)
+    for i, (dy, dz) in enumerate(DP_OFFSETS):
+        owner = dp_dev(dy, dz)
+        pltpu.make_async_remote_copy(
+            mass_send.at[owner // (LANES // 8)], mass_recv.at[i], mass_sems.at[0], mass_sems.at[1],
+            device_id=(owner, cl), device_id_type=MESH,
+        ).start()
+
+    for slot in (2, 3):
         for ch in range(CHUNKS):
             for h in range(2):
                 for way in range(2):
-                    ring_take(h, ch, way, s)
-                    ring_send(h, ch, way, s + 1)
+                    if slot == 2:
+                        ring_take(h, ch, way, 0)
+                    ring_take(h, ch, way, slot - 1)
+                    ring_send(h, ch, way, slot)
     for ch in range(CHUNKS):
         for h in range(2):
             for way in range(2):
-                ring_take(h, ch, way, STEPS)
+                ring_take(h, ch, way, 3)
             red[h, ch] = num[h, ch, place[h]]
             for d in RING_OFFSETS:
                 pltpu.make_async_remote_copy(
@@ -256,7 +260,7 @@
             pltpu.VMEM((K, N), f32),
             pltpu.VMEM((K, N), jnp.bfloat16),
             pltpu.VMEM((2, CHUNKS, 8, 8, 8, W), f32),
-            pltpu.VMEM((2, 2, CHUNKS, STEPS, 8, 8, W), f32),
+            pltpu.VMEM((2, 2, CHUNKS, SLOTS, 8, 8, W), f32),
             pltpu.VMEM((2, CHUNKS, 8, 8, W), f32),
             pltpu.VMEM((2, CHUNKS, 7, 8, W), f32),
             pltpu.VMEM((ITERS, T, LANES), f32),
@@ -272,7 +276,7 @@
             dma((ITERS,)),
             dma((2,)),
             dma((2, 2, CHUNKS)),
-            dma((2, 2, CHUNKS, STEPS)),
+            dma((2, 2, CHUNKS, SLOTS)),
             dma((2, CHUNKS)),
             dma((2, CHUNKS)),
         ],

time: 75.9 us -> 72.7 us (0.958)
  the two profiles are of different devices: /device:TPU:8 before, /device:TPU:1 now
where the time goes in v3:
time: 72.7 us; the launch traced here: 71.9 us
  Pallas kernels  71.2 us (98%)
    pallas_call x1, Pallas kernels, per_device(): pl.pallas_call(main_kernel, out_shape=jax.ShapeDtypeStruct((D // LANES +...  70.6 us

profile of v3, /device:TPU:1, one launch (start us, length us, event | category | flops | bytes accessed | tf_op | source)
XLA Modules:
  0.0 71.9 jit_solution(4943553209110235341)
XLA Ops:
  0.6 70.6 %shard_map.49.all_ref = f32[9,8,128]{2,1,0:T(8,128)S(1)} custom-call(bf16[512,1024]{1,0:T(8,128)(2,1)} %e_hbm.1, bf16[512,1024]{1,0:T(8,128)(2,1)} %c_hbm.1), custom_call_target="tpu_custom_call" | custom-call | tf_op jit(solution)/shard_map/pallas_call | solution.py:251
  71.2 0.6 shard_map.50

commit v4 on v3

--- a/solution.py
+++ b/solution.py
@@ -18,6 +18,8 @@
 CHUNKS = 4
 W = HALF // CHUNKS
 SLOTS = 4
+GROUP = 2
+GROUPS = CHUNKS // GROUP
 VMEM_LIMIT = 267 * 2**20 // 5
 MESH = pl.DeviceIdType.MESH
 
@@ -50,15 +52,18 @@
 def main_kernel(
     e_hbm, c_hbm, out_ref,
     e_ref, cent_ref, s_ref, st_ref, plan_ref, num, got, red, fin,
-    col_send, col_recv, row_send, row_recv, mass_send, mass_recv,
+    col_send, col_recv, row_send, row_recv, mass_send, mass_part, mass_recv,
     load_sem, col_ssem, col_rsem, row_ssem, row_rsem, mass_sems, ring_ssem, ring_rsem, fin_ssem, fin_rsem,
 ):
     dp = lax.axis_index("dp")
     cl = lax.axis_index("cluster")
     y, z = dp // NZ, lax.rem(dp, NZ)
 
+    row_start = [lax.rem(y + d, NY) * NZ for d in range(NY)]
+    in_row = [lax.rem(z + d, NZ) for d in range(NZ)]
+
     def dp_dev(dy, dz):
-        return lax.rem(y + dy, NY) * NZ + lax.rem(z + dz, NZ)
+        return row_start[dy] + in_row[dz]
 
     load_e = pltpu.make_async_copy(e_hbm, e_ref, load_sem.at[0])
     load_c = pltpu.make_async_copy(c_hbm, cent_ref, load_sem.at[1])
@@ -75,32 +80,38 @@
     load_c.wait()
     nt = (((1,), (1,)), ((), ()))
 
-    def score_rows(j, _):
-        rows = pl.ds(pl.multiple_of(j * LANES, LANES), LANES)
-        st_ref[rows, :] = jnp.exp(
-            lax.dot_general(cent_ref[rows, :], e_ref[...], nt, preferred_element_type=jnp.float32) * INV_TEMP
-        )
-        s_ref[rows, :] = jnp.exp(
-            lax.dot_general(e_ref[rows, :], cent_ref[...], nt, preferred_element_type=jnp.float32) * INV_TEMP
-        )
-        return 0
-
-    lax.fori_loop(0, T, score_rows, 0)
-    pl.semaphore_wait(barrier, len(DP_OFFSETS) + len(CL_OFFSETS))
+    def scores(left, right, to):
+        def block(j, _):
+            rows = pl.ds(pl.multiple_of(j * LANES, LANES), LANES)
+            to[rows, :] = jnp.exp(
+                lax.dot_general(left[rows, :], right[...], nt, preferred_element_type=jnp.float32) * INV_TEMP
+            )
+            return 0
+
+        lax.fori_loop(0, T, block, 0)
+
+    scores(cent_ref, e_ref, st_ref)
 
     def total_wait(buf, sem):
         pltpu.make_async_copy(buf, buf, sem).wait()
 
-    def iteration(it, r):
+    def column_sums(it, r):
         def put_col(j, v):
             col_send[it, j : j + 1, :] = v
 
         weighted_sums(st_ref, r, put_col)
+
+    column_sums(0, jnp.ones((T, LANES), jnp.float32))
+    pl.semaphore_wait(barrier, len(DP_OFFSETS) + len(CL_OFFSETS))
+
+    def iteration(it):
         for i, (dy, dz) in enumerate(DP_OFFSETS):
             pltpu.make_async_remote_copy(
                 col_send.at[it], col_recv.at[it, i], col_ssem.at[it], col_rsem.at[it],
                 device_id=(dp_dev(dy, dz), cl), device_id_type=MESH,
             ).start()
+        if it == 0:
+            scores(e_ref, cent_ref, s_ref)
         total_wait(col_recv.at[it], col_rsem.at[it])
         c = RATIO / (col_send[it] + jnp.sum(col_recv[it], axis=0))
         out_ref[NZ, T : 2 * T, :] = c
@@ -115,8 +126,7 @@
                 device_id=(dp, lax.rem(cl + j, NCL)), device_id_type=MESH,
             ).start()
 
-        @pl.when(it == ITERS - 1)
-        def _():
+        if it == ITERS - 1:
             for j in range(T):
                 rows = slice(j * LANES, (j + 1) * LANES)
                 c_col = jnp.broadcast_to(c[j : j + 1, :], (LANES, LANES)).T
@@ -125,9 +135,14 @@
                     st_ref[rows, cols] = st_ref[rows, cols] * c_col
 
         total_wait(row_recv.at[it], row_rsem.at[it])
-        return 1.0 / (row_send[it] + jnp.sum(row_recv[it], axis=0))
-
-    r = lax.fori_loop(0, ITERS, iteration, jnp.ones((T, LANES), jnp.float32))
+        r = 1.0 / (row_send[it] + jnp.sum(row_recv[it], axis=0))
+
+        if it < ITERS - 1:
+            column_sums(it + 1, r)
+        return r
+
+    for it in range(ITERS):
+        r = iteration(it)
     out_ref[NZ, 0:T, :] = r
 
     for j in range(T):
@@ -158,7 +173,7 @@
         owner, part = ring_owner(h, way, 4 - slot), ring_part(way, slot)
         pltpu.make_async_remote_copy(
             num.at[h, ch, owner, part], got.at[h, way, ch, slot, part],
-            ring_ssem.at[h, way, ch], ring_rsem.at[h, way, ch, slot],
+            ring_ssem.at[h, way], ring_rsem.at[h, way, ch, slot],
             device_id=device_at(h, 8 - hops if way == 0 else hops, True), device_id_type=MESH,
         ).start()
 
@@ -167,25 +182,28 @@
         total_wait(got.at[h, way, ch, slot, part], ring_rsem.at[h, way, ch, slot])
         num[h, ch, ring_owner(h, way, min(2, 3 - slot)), part] += got[h, way, ch, slot, part]
 
-    for ch in range(CHUNKS):
+    for g in range(GROUPS):
         for h in range(2):
-            cols = slice(h * HALF + ch * W, h * HALF + (ch + 1) * W)
-            block = jnp.dot(plan_ref[...], e_ref[:, cols], preferred_element_type=jnp.float32).reshape(8, 8, 8, W)
-            if h == 0:
-                num[h, ch] = block
-            else:
-                for k in range(8):
-                    num[h, ch, :, k] = block[k]
-            for slot in range(2):
-                for way in range(2):
-                    ring_send(h, ch, way, slot)
-    for i, (dy, dz) in enumerate(DP_OFFSETS):
-        owner = dp_dev(dy, dz)
+            first = h * HALF + g * GROUP * W
+            block = jnp.dot(
+                plan_ref[...], e_ref[:, first : first + GROUP * W], preferred_element_type=jnp.float32
+            ).reshape(8, 8, 8, GROUP * W)
+            for i in range(GROUP):
+                ch, part = g * GROUP + i, block[..., i * W : (i + 1) * W]
+                if h == 0:
+                    num[h, ch] = part
+                else:
+                    for k in range(8):
+                        num[h, ch, :, k] = part[k]
+                for slot in range(2):
+                    for way in range(2):
+                        ring_send(h, ch, way, slot)
+    for d in RING_OFFSETS:
+        owner = dp_dev(d, 0)
         pltpu.make_async_remote_copy(
-            mass_send.at[owner // (LANES // 8)], mass_recv.at[i], mass_sems.at[0], mass_sems.at[1],
+            mass_send.at[owner // (LANES // 8)], mass_recv.at[0, d - 1], mass_sems.at[0], mass_sems.at[1],
             device_id=(owner, cl), device_id_type=MESH,
         ).start()
-
     for slot in (2, 3):
         for ch in range(CHUNKS):
             for h in range(2):
@@ -194,40 +212,51 @@
                         ring_take(h, ch, way, 0)
                     ring_take(h, ch, way, slot - 1)
                     ring_send(h, ch, way, slot)
-    for ch in range(CHUNKS):
+    total_wait(mass_recv.at[0], mass_sems.at[1])
+    mass_part[...] = mass_send[dp // (LANES // 8)] + jnp.sum(mass_recv[0], axis=0)
+    for d in RING_OFFSETS:
+        pltpu.make_async_remote_copy(
+            mass_part, mass_recv.at[1, d - 1], mass_sems.at[2], mass_sems.at[3],
+            device_id=(dp_dev(0, d), cl), device_id_type=MESH,
+        ).start()
+    for g in range(GROUPS):
         for h in range(2):
-            for way in range(2):
-                ring_take(h, ch, way, 3)
-            red[h, ch] = num[h, ch, place[h]]
+            for i in range(GROUP):
+                ch = g * GROUP + i
+                for way in range(2):
+                    total_wait(got.at[h, way, ch, 3], ring_rsem.at[h, way, ch, 3])
+                red[h, g, :, i] = num[h, ch, place[h]] + got[h, 0, ch, 3] + got[h, 1, ch, 3]
             for d in RING_OFFSETS:
                 pltpu.make_async_remote_copy(
-                    red.at[h, ch, lax.rem(other[h] + d, 8)], fin.at[h, ch, d - 1], fin_ssem.at[h, ch], fin_rsem.at[h, ch],
+                    red.at[h, g, lax.rem(other[h] + d, 8)], fin.at[h, g, d - 1], fin_ssem.at[h], fin_rsem.at[h, g],
                     device_id=device_at(h, d, False), device_id_type=MESH,
                 ).start()
 
-    total_wait(mass_recv, mass_sems.at[1])
-    mass_row = mass_send[dp // (LANES // 8)] + jnp.sum(mass_recv[...], axis=0)
+    for it in range(ITERS):
+        total_wait(col_recv.at[it], col_ssem.at[it])
+        total_wait(row_recv.at[it], row_ssem.at[it])
+    total_wait(mass_recv.at[0], mass_sems.at[0])
+    for h in range(2):
+        for way in range(2):
+            total_wait(got.at[h, way, :, pl.ds(0, 3)], ring_ssem.at[h, way])
+            total_wait(got.at[h, way, :, 3, pl.ds(0, 4)], ring_ssem.at[h, way])
+
+    total_wait(mass_recv.at[1], mass_sems.at[3])
+    total_wait(mass_recv.at[1], mass_sems.at[2])
+    mass_row = mass_part[...] + jnp.sum(mass_recv[1], axis=0)
     mine = lax.broadcasted_iota(jnp.int32, (8, LANES), 1) == (
         lax.rem(dp, LANES // 8) * 8 + lax.broadcasted_iota(jnp.int32, (8, LANES), 0)
     )
     mass = jnp.sum(jnp.where(mine, jnp.broadcast_to(mass_row, (8, LANES)), 0.0), axis=1, keepdims=True)
-    for ch in range(CHUNKS):
+    for g in range(GROUPS):
         for h in range(2):
-            total_wait(fin.at[h, ch], fin_rsem.at[h, ch])
-            block = (red[h, ch, other[h]] + jnp.sum(fin[h, ch], axis=0)) / mass
-            for q in range(W // LANES):
-                out_ref[(h * HALF + ch * W) // LANES + q] = block[:, q * LANES : (q + 1) * LANES]
-
-    for it in range(ITERS):
-        total_wait(col_recv.at[it], col_ssem.at[it])
-        total_wait(row_recv.at[it], row_ssem.at[it])
-    total_wait(mass_recv, mass_sems.at[0])
+            total_wait(fin.at[h, g], fin_rsem.at[h, g])
+            for i in range(GROUP):
+                block = (red[h, g, other[h], i] + jnp.sum(fin[h, g, :, i], axis=0)) / mass
+                for q in range(W // LANES):
+                    out_ref[(h * HALF + (g * GROUP + i) * W) // LANES + q] = block[:, q * LANES : (q + 1) * LANES]
     for h in range(2):
-        for ch in range(CHUNKS):
-            total_wait(fin.at[h, ch], fin_ssem.at[h, ch])
-            for way in range(2):
-                total_wait(got.at[h, way, ch, pl.ds(0, 3)], ring_ssem.at[h, way, ch])
-                total_wait(got.at[h, way, ch, 3, pl.ds(0, 4)], ring_ssem.at[h, way, ch])
+        total_wait(fin.at[h], fin_ssem.at[h])
 
 
 def finish_kernel(all_ref, out_ref, lr_ref, lc_ref):
@@ -261,24 +290,25 @@
             pltpu.VMEM((K, N), jnp.bfloat16),
             pltpu.VMEM((2, CHUNKS, 8, 8, 8, W), f32),
             pltpu.VMEM((2, 2, CHUNKS, SLOTS, 8, 8, W), f32),
-            pltpu.VMEM((2, CHUNKS, 8, 8, W), f32),
-            pltpu.VMEM((2, CHUNKS, 7, 8, W), f32),
+            pltpu.VMEM((2, GROUPS, 8, GROUP, 8, W), f32),
+            pltpu.VMEM((2, GROUPS, 7, GROUP, 8, W), f32),
             pltpu.VMEM((ITERS, T, LANES), f32),
             pltpu.VMEM((ITERS, n_dp, T, LANES), f32),
             pltpu.VMEM((ITERS, T, LANES), f32),
             pltpu.VMEM((ITERS, n_cl, T, LANES), f32),
             pltpu.VMEM((T, 1, LANES), f32),
-            pltpu.VMEM((n_dp, 1, LANES), f32),
+            pltpu.VMEM((1, LANES), f32),
+            pltpu.VMEM((2, 7, 1, LANES), f32),
             dma((2,)),
             dma((ITERS,)),
             dma((ITERS,)),
             dma((ITERS,)),
             dma((ITERS,)),
+            dma((4,)),
+            dma((2, 2)),
+            dma((2, 2, CHUNKS, SLOTS)),
             dma((2,)),
-            dma((2, 2, CHUNKS)),
-            dma((2, 2, CHUNKS, SLOTS)),
-            dma((2, CHUNKS)),
-            dma((2, CHUNKS)),
+            dma((2, GROUPS)),
         ],
         compiler_params=pltpu.CompilerParams(
             collective_id=0, has_side_effects=True, vmem_limit_bytes=VMEM_LIMIT

time: 72.7 us -> 72.1 us (level)
  Pallas kernels: 71.2 us -> 70.3 us
    pallas_call x1, Pallas kernels: 70.6 us -> 69.7 us  [per_device(): pl.pallas_call(main_kernel, out_shape=jax.ShapeDtypeStruct((D // LANES +...]
where the time goes in v4:
time: 72.1 us; the launch traced here: 70.9 us
  Pallas kernels  70.3 us (98%)
    pallas_call x1, Pallas kernels, per_device(): pl.pallas_call(main_kernel, out_shape=jax.ShapeDtypeStruct((D // LANES +...  69.7 us

profile of v4, /device:TPU:1, one launch (start us, length us, event | category | flops | bytes accessed | tf_op | source)
XLA Modules:
  0.0 70.9 jit_solution(8178741916749113182)
XLA Ops:
  0.6 69.7 %shard_map.49.all_ref = f32[9,8,128]{2,1,0:T(8,128)S(1)} custom-call(bf16[512,1024]{1,0:T(8,128)(2,1)} %e_hbm.1, bf16[512,1024]{1,0:T(8,128)(2,1)} %c_hbm.1), custom_call_target="tpu_custom_call" | custom-call | tf_op jit(solution)/shard_map/pallas_call | solution.py:280
  70.3 0.6 shard_map.50

commit v5 on v4

--- a/solution.py
+++ b/solution.py
@@ -162,25 +162,21 @@
         shift = (step, 0) if (h == 0) == along else (0, step)
         return (dp_dev(*shift), cl)
 
-    def ring_part(way, slot):
-        return pl.ds(4 * way, 4) if slot == 0 else pl.ds(0, 8)
-
     def ring_owner(h, way, distance):
         return lax.rem(place[h] + (8 - distance if way == 0 else distance), 8)
 
     def ring_send(h, ch, way, slot):
         hops = 2 if slot == 0 else 1
-        owner, part = ring_owner(h, way, 4 - slot), ring_part(way, slot)
+        owner = ring_owner(h, way, 4 - slot)
         pltpu.make_async_remote_copy(
-            num.at[h, ch, owner, part], got.at[h, way, ch, slot, part],
+            num.at[h, ch, owner], got.at[h, way, ch, slot],
             ring_ssem.at[h, way], ring_rsem.at[h, way, ch, slot],
             device_id=device_at(h, 8 - hops if way == 0 else hops, True), device_id_type=MESH,
         ).start()
 
     def ring_take(h, ch, way, slot):
-        part = ring_part(way, slot)
-        total_wait(got.at[h, way, ch, slot, part], ring_rsem.at[h, way, ch, slot])
-        num[h, ch, ring_owner(h, way, min(2, 3 - slot)), part] += got[h, way, ch, slot, part]
+        total_wait(got.at[h, way, ch, slot], ring_rsem.at[h, way, ch, slot])
+        num[h, ch, ring_owner(h, way, min(2, 3 - slot))] += got[h, way, ch, slot]
 
     for g in range(GROUPS):
         for h in range(2):
@@ -197,7 +193,8 @@
                         num[h, ch, :, k] = part[k]
                 for slot in range(2):
                     for way in range(2):
-                        ring_send(h, ch, way, slot)
+                        if slot or way == ch % 2:
+                            ring_send(h, ch, way, slot)
     for d in RING_OFFSETS:
         owner = dp_dev(d, 0)
         pltpu.make_async_remote_copy(
@@ -208,7 +205,7 @@
         for ch in range(CHUNKS):
             for h in range(2):
                 for way in range(2):
-                    if slot == 2:
+                    if slot == 2 and way == ch % 2:
                         ring_take(h, ch, way, 0)
                     ring_take(h, ch, way, slot - 1)
                     ring_send(h, ch, way, slot)
@@ -239,7 +236,7 @@
     for h in range(2):
         for way in range(2):
             total_wait(got.at[h, way, :, pl.ds(0, 3)], ring_ssem.at[h, way])
-            total_wait(got.at[h, way, :, 3, pl.ds(0, 4)], ring_ssem.at[h, way])
+            total_wait(got.at[h, way, pl.ds(0, CHUNKS // 2), 3], ring_ssem.at[h, way])
 
     total_wait(mass_recv.at[1], mass_sems.at[3])
     total_wait(mass_recv.at[1], mass_sems.at[2])

time: 72.1 us -> 72.4 us (level)
  no operation moved by 1% of the time
where the time goes in v5:
time: 72.4 us; the launch traced here: 71 us
  Pallas kernels  70.4 us (97%)
    pallas_call x1, Pallas kernels, per_device(): pl.pallas_call(main_kernel, out_shape=jax.ShapeDtypeStruct((D // LANES +...  69.8 us

profile of v5, /device:TPU:1, one launch (start us, length us, event | category | flops | bytes accessed | tf_op | source)
XLA Modules:
  0.0 71.0 jit_solution(10684755498474917592)
XLA Ops:
  0.6 69.8 %shard_map.49.all_ref = f32[9,8,128]{2,1,0:T(8,128)S(1)} custom-call(bf16[512,1024]{1,0:T(8,128)(2,1)} %e_hbm.1, bf16[512,1024]{1,0:T(8,128)(2,1)} %c_hbm.1), custom_call_target="tpu_custom_call" | custom-call | tf_op jit(solution)/shard_map/pallas_call | solution.py:277
  70.4 0.6 shard_map.50
